TPU v7x, 32 devices: a whole 2x2x4 slice. The times are simulated.
32 devices in a mesh: tok: 4 (over y, x), blk: 8 (over z, core).
Axes of the slice: x: 2, y: 2, z: 4, core: 2. Of those that a mesh axis runs over, the one named last changes fastest.
Arguments:
- features: bfloat16 [2048, 8192], P('tok'), may hold values from -6 to 6
- hidden_grad: bfloat16 [2048, 28672], P('tok', 'blk'), may hold values from -0.125 to 0.125
- block_mask: int32 [64, 224], replicated, may hold values from 0 to 1, as said below
- old_columns: int32 [8, 28], replicated, may hold values from 0 to 224, as said below
- new_columns: int32 [8, 28], replicated, may hold values from 0 to 224, as said below
- weights: float32 [4, 224, 8, 128, 128], P('tok', 'blk'), may hold values from -0.75 to 0.75
- first_moment: float32 [4, 224, 8, 128, 128], P('tok', 'blk'), may hold values from -6 to 6
- second_moment: float32 [4, 224, 8, 128, 128], P('tok', 'blk'), may hold values from 0.001 to 1
Outputs:
- new_weights: float32 [4, 224, 8, 128, 128], P('tok', 'blk')
- new_first: float32 [4, 224, 8, 128, 128], P('tok', 'blk')
- new_second: float32 [4, 224, 8, 128, 128], P('tok', 'blk')
Inputs may be any that keep to these rules, and one draw needn't show every extreme that they name: `block_mask`: in every column, each aligned group of 16 row blocks holds at most 8 ones; some group holds exactly 8. `old_columns`: every column number below 224 stands exactly once; all other entries are 224. `new_columns`: equal to old_columns except that, for some owners k, the entries [k, 0] and [(k + 1) mod 8, 27] of old_columns are exchanged.
All inputs are finite; a program needn't handle non-finite values.
Results may differ from a plain program's by a relative error of at most 0.0003.
Values may be sent and summed in bfloat16 or wider, within the bound.
A program may use at most 448 MiB of HBM per device.

v0:
```python
import jax
import jax.numpy as jnp
from jax import lax
from jax.sharding import PartitionSpec as P

beta_one = 0.9
beta_two = 0.95
learn_rate = 0.05
weight_decay = 0.1
adam_eps = 1e-08
adam_steps = 20.0


def passed_along(value, axis, steps):
    count = lax.axis_size(axis)
    pairs = [(source, (source + steps) % count) for source in range(count)]
    return lax.ppermute(value, axis, pairs)


def block_rows(block_mask, columns, first_row, range_rows, capacity):
    total_cols = block_mask.shape[1]
    window = lax.dynamic_slice_in_dim(block_mask, first_row, range_rows, 0)
    selector = (columns[:, None] == jnp.arange(total_cols, dtype=jnp.int32)[None, :]).astype(
        jnp.int32
    )
    present = jnp.sum(selector[:, None, :] * window[None, :, :], axis=2)
    running = jnp.cumsum(present, axis=1)
    places = jnp.arange(capacity, dtype=jnp.int32)
    local_rows = jnp.arange(range_rows, dtype=jnp.int32)
    matches = (present[:, None, :] == 1) & (running[:, None, :] == places[None, :, None] + 1)
    row_ids = jnp.sum(jnp.where(matches, local_rows[None, None, :], 0), axis=2)
    usable = (running[:, -1:] > places[None, :]).astype(jnp.float32)
    return (row_ids, usable)


def adam_update(weights, moment_one, moment_two, gradient):
    first_new = beta_one * moment_one + (1.0 - beta_one) * gradient
    second_new = beta_two * moment_two + (1.0 - beta_two) * gradient * gradient
    fix_one = 1.0 - beta_one**adam_steps
    fix_two = 1.0 - beta_two**adam_steps
    update = first_new / fix_one / (jnp.sqrt(second_new / fix_two) + adam_eps)
    stepped = weights - learn_rate * (update + weight_decay * weights)
    return (stepped, first_new, second_new)


def slot_gradient(features, hidden_grad, block_mask, columns, capacity):
    ranges = lax.axis_size("tok")
    total_rows = block_mask.shape[0]
    range_rows = total_rows // ranges
    slot_count = columns.shape[0]
    block_width = hidden_grad.shape[1] // slot_count
    tok_rows = features.shape[0]
    starts = jnp.arange(ranges, dtype=jnp.int32) * range_rows

    def rows_for(range_start):
        return block_rows(block_mask, columns, range_start, range_rows, capacity)

    local_ids, usable = jax.vmap(rows_for)(starts)
    global_ids = local_ids + starts[:, None, None]
    token_blocks = features.reshape(tok_rows, total_rows, block_width)
    hidden_cols = hidden_grad.reshape(tok_rows, slot_count, block_width)
    group_rows = slot_count * capacity
    pieces = group_rows * lax.axis_size("tok") // group_rows
    token_tiles = jnp.take(token_blocks, global_ids.reshape(-1), axis=1)
    token_tiles = token_tiles.reshape(tok_rows, pieces, slot_count, capacity, block_width)
    product = jnp.einsum(
        "tacki,tcj->ackij", token_tiles, hidden_cols, preferred_element_type=jnp.float32
    )
    product = product * usable[:, :, :, None, None]
    summed = lax.psum_scatter(
        product.reshape(group_rows * lax.axis_size("tok"), block_width, block_width),
        "tok",
        scatter_dimension=0,
        tiled=True,
    )
    return summed.reshape(slot_count, capacity, block_width, block_width)


def slot_flags(old_columns, new_columns):
    owner_index = lax.axis_index("blk")
    last_slot = old_columns.shape[1] - 1
    old_mine = lax.dynamic_index_in_dim(old_columns, owner_index, 0, keepdims=False)
    new_mine = lax.dynamic_index_in_dim(new_columns, owner_index, 0, keepdims=False)
    into_first = new_mine[0] != old_mine[0]
    into_last = new_mine[last_slot] != old_mine[last_slot]
    return (old_mine, new_mine, into_first, into_last)


def relocate(weights, moment_one, moment_two, into_first, into_last):
    last_slot = weights.shape[0] - 1
    from_lower = passed_along((weights[0], moment_one[0], moment_two[0]), "blk", 1)
    from_upper = passed_along(
        (weights[last_slot], moment_one[last_slot], moment_two[last_slot]), "blk", -1
    )
    relocated = []
    for state_now, lower_piece, upper_piece in zip(
        (weights, moment_one, moment_two), from_lower, from_upper
    ):
        head_tile = jnp.where(into_first, upper_piece, state_now[0])
        tail_tile = jnp.where(into_last, lower_piece, state_now[last_slot])
        relocated.append(
            jnp.concatenate([head_tile[None], state_now[1:last_slot], tail_tile[None]], axis=0)
        )
    return (relocated[0], relocated[1], relocated[2])


def body(
    features,
    hidden_grad,
    block_mask,
    old_columns,
    new_columns,
    weights,
    first_moment,
    second_moment,
):
    capacity = weights.shape[2]
    range_rows = block_mask.shape[0] // lax.axis_size("tok")
    tok_index = lax.axis_index("tok")
    old_mine, new_mine, into_first, into_last = slot_flags(old_columns, new_columns)
    gradient = slot_gradient(features, hidden_grad, block_mask, old_mine, capacity)
    stepped, first_new, second_new = adam_update(
        weights[0], first_moment[0], second_moment[0], gradient
    )
    stepped, first_new, second_new = relocate(stepped, first_new, second_new, into_first, into_last)
    unused_rows, usable = block_rows(
        block_mask, new_mine, tok_index * range_rows, range_rows, capacity
    )
    keep_mask = usable[:, :, None, None]
    return (
        (stepped * keep_mask)[None],
        (first_new * keep_mask)[None],
        (second_new * keep_mask)[None],
    )


def solution(mesh):
    return jax.shard_map(
        body,
        mesh=mesh,
        in_specs=(
            P("tok", None),
            P("tok", "blk"),
            P(),
            P(),
            P(),
            P("tok", "blk", None, None, None),
            P("tok", "blk", None, None, None),
            P("tok", "blk", None, None, None),
        ),
        out_specs=(
            P("tok", "blk", None, None, None),
            P("tok", "blk", None, None, None),
            P("tok", "blk", None, None, None),
        ),
        check_vma=False,
    )
```

profile of v0, /device:TPU:0, one launch (start us, length us, event | category | flops | bytes accessed | tf_op | source)
XLA Modules:
  0.0 1007.5 jit_solution(17667847388641265745)
XLA Ops:
  9.1 7.9 while.1
  17.0 2.0 multiply_reduce_fusion
  20.5 11.9 %copy.42 = bf16[512,8192]{0,1:T(8,128)(2,1)} copy(bf16[512,8192]{1,0:T(8,128)(2,1)} %param.8) | data formatting | bytes 16777216 | tf_op args[0]
  32.4 11.9 %copy.44 = bf16[512,64,128]{2,0,1:T(8,128)(2,1)} copy(bf16[512,64,128]{0,2,1:T(8,128)(2,1)} %bitcast.83) | data formatting | bytes 16777216 | tf_op jit(solution)/shard_map/reshape | solution.py:60
  44.3 44.1 %gather_fusion = bf16[896,512,128]{2,1,0:T(8,128)(2,1)} fusion(bf16[512,64,128]{2,0,1:T(8,128)(2,1)} %copy.44, s32[1024]{0:T(1024)S(1)} %pad_clamp_fusion), kind=kCustom, calls=%fused_computation | custom fusion | bytes 234884608 | tf_op jit(solution)/shard_map/jit(_take)/gather | solution.py:64
  88.4 96.0 %copy.45 = bf16[512,896,128]{2,1,0:T(8,128)(2,1)} copy(bf16[512,896,128]{2,0,1:T(8,128)(2,1)} %bitcast.5) | data formatting | bytes 234881024 | tf_op jit(solution)/shard_map/jit(_take)/gather | solution.py:64
  185.0 5.9 copy.46
  190.9 75.7 %broadcast_select_fusion = bf16[512,4,28,8,128]{4,3,2,1,0:T(8,128)(2,1)} fusion(bf16[512,4,28,8,128]{4,3,2,1,0:T(8,128)(2,1)} %bitcast.6, pred[4,28,8]{2,1,0:T(8,128)(4,1)S(1)} %copy.41), kind=kLoop, calls=%fused_computation.5 | loop fusion | flops 58720256 | bytes 234881920 | tf_op jit(solution)/shard_map/jit(_take)/select_n | solution.py:64
  266.7 70.0 %bitcast_multiply_fusion = f32[4,28,8,128,128]{4,3,2,0,1:T(8,128)} fusion(f32[4,28,8]{2,0,1:T(4,128)S(1)} %fusion.7, bf16[512,28,128,1,1]{0,2,4,3,1:T(8,128)(2,1)} %bitcast.85, bf16[512,4,28,8,128]{4,3,2,1,0:T(8,128)(2,1)} %broadcast_select_fusion), kind=kOutput, calls=%fused_computation.6 | convolution fusion | flops 15047065600 | bytes 179834368 | tf_op jit(solution)/shard_map/tacki,tcj->ackij/dot_general | solution.py:66
  336.7 38.3 %copy.50 = f32[4,28,8,128,128]{4,3,2,1,0:T(8,128)} copy(f32[4,28,8,128,128]{4,3,2,0,1:T(8,128)} %bitcast_multiply_fusion) | data formatting | bytes 117440512 | tf_op jit(solution)/shard_map/mul | solution.py:69
  380.9 489.1 %reduce-scatter.2.cloned.1.call-done = f32[224,128,128]{2,1,0:T(8,128)} async-done(((f32[896,128,128]{2,1,0:T(8,128)}), f32[224,128,128]{2,1,0:T(8,128)}) %reduce-scatter.2.cloned.1.call-update) | async-done | bytes 14680080 | tf_op jit(solution)/shard_map/reduce_scatter | solution.py:70
  870.0 35.4 %bitcast_subtract_fusion = (f32[28,8,128,128]{3,2,1,0:T(8,128)}, f32[28,8,128,128]{3,2,1,0:T(8,128)}, f32[28,8,128,128]{3,2,1,0:T(8,128)}) fusion(f32[1,28,8,128,128]{4,3,2,1,0:T(8,128)} %param.13, f32[28,8,128,128]{3,2,1,0:T(8,128)} %bitcast.84, f32[1,28,8,128,128]{4,3,2,1,0:T(8,128)} %param.14, f32[1,28,8,128,128]{4,3,2,1,0:T(8,128)} %param.15), kind=kLoop, calls=%fused_computation.13 | loop fusion | flops 55050240 | bytes 102760448 | tf_op jit(solution)/shard_map/sub | solution.py:42
  906.7 12.2 %slice_bitcast_fusion.1 = f32[1,26,8,128,128]{4,3,2,1,0:T(8,128)} fusion(f32[28,8,128,128]{3,2,1,0:T(8,128)} %get-tuple-element.20), kind=kLoop, calls=%fused_computation.18 | loop fusion | bytes 27262976 | tf_op jit(solution)/shard_map/concatenate | solution.py:102
  918.9 2.1 slice_bitcast_fusion.8
  921.0 12.2 %slice_bitcast_fusion.2 = f32[1,26,8,128,128]{4,3,2,1,0:T(8,128)} fusion(f32[28,8,128,128]{3,2,1,0:T(8,128)} %get-tuple-element.19), kind=kLoop, calls=%fused_computation.19 | loop fusion | bytes 27262976 | tf_op jit(solution)/shard_map/concatenate | solution.py:102
  933.2 2.8 collective-permute-start
  936.0 3.5 collective-permute-start.2
  939.5 12.1 %slice_bitcast_fusion = f32[1,26,8,128,128]{4,3,2,1,0:T(8,128)} fusion(f32[28,8,128,128]{3,2,1,0:T(8,128)} %get-tuple-element.21), kind=kLoop, calls=%fused_computation.17 | loop fusion | bytes 27262976 | tf_op jit(solution)/shard_map/concatenate | solution.py:102
  952.9 3.6 collective-permute-start.4
  958.0 1.8 collective-permute-done.2
  959.8 3.5 collective-permute-done.3
  964.6 4.3 collective-permute-done.4
  968.9 3.1 collective-permute-done.5
  973.3 27.3 %maximum_multiply_fusion.2 = (f32[1,28,8,128,128]{4,3,2,1,0:T(8,128)}, f32[1,28,8,128,128]{4,3,2,1,0:T(8,128)}, f32[1,28,8,128,128]{4,3,2,1,0:T(8,128)}) fusion(f32[1,1,8,128,128]{4,3,2,1,0:T(8,128)S(1)} %get-tuple-element.25, f32[1,26,8,128,128]{4,3,2,1,0:T(8,128)} %slice_bitcast_fusion, f32[1,1,8,128,128]{4,3,2,1,0:T(8,128)S(1)} %get-tuple-element.24, ...), kind=kLoop, calls=%fused_computation.11 | loop fusion | flops 33030144 | bytes 88081280 | tf_op jit(solution)/shard_map/mul | solution.py:133
  (57 shorter events, 21.7 us)
Async XLA Ops:
  7.2 862.8 %reduce-scatter.2.cloned.1.call-start = ((), (), s32[]{:S(2)}) async-start(), calls=%async_computation.1 | async-start | bytes 73400320 | tf_op jit(solution)/shard_map/reduce_scatter | solution.py:70
  8.5 0.5 copy-start.1
  375.0 0.6 copy-start.2
  375.0 1.3 copy-start
  933.2 23.3 %collective-permute-start = (f32[8,128,128]{2,1,0:T(8,128)}, f32[8,128,128]{2,1,0:T(8,128)S(1)}, u32[]{:S(2)}, u32[]{:S(2)}) collective-permute-start(f32[8,128,128]{2,1,0:T(8,128)} %get-tuple-element.34), channel_id=1, source_target_pairs={{0,7},{1,0},{2,1},{3,2},{4,3},{5,4},{6,5},{7,6},{8,15},{9,8},{10,9... | collective-permute-start | bytes 1572872 | tf_op jit(solution)/shard_map/ppermute | solution.py:17
  936.0 20.6 %collective-permute-start.1 = (f32[8,128,128]{2,1,0:T(8,128)S(1)}, f32[8,128,128]{2,1,0:T(8,128)}, u32[]{:S(2)}, u32[]{:S(2)}) collective-permute-start(f32[8,128,128]{2,1,0:T(8,128)S(1)} %get-tuple-element.35), channel_id=1, source_target_pairs={{0,1},{1,2},{2,3},{3,4},{4,5},{5,6},{6,7},{7,0},{8,9},{9,10},{10,1... | collective-permute-start | bytes 1572872 | tf_op jit(solution)/shard_map/ppermute | solution.py:17
  936.0 23.8 %collective-permute-start.2 = (f32[8,128,128]{2,1,0:T(8,128)S(1)}, f32[8,128,128]{2,1,0:T(8,128)S(1)}, u32[]{:S(2)}, u32[]{:S(2)}) collective-permute-start(f32[8,128,128]{2,1,0:T(8,128)S(1)} %get-tuple-element.30), channel_id=1, source_target_pairs={{0,7},{1,0},{2,1},{3,2},{4,3},{5,4},{6,5},{7,6},{8,15},{9,8},{10,9... | collective-permute-start | bytes 1572872 | tf_op jit(solution)/shard_map/ppermute | solution.py:17
  939.5 23.8 %collective-permute-start.3 = (f32[8,128,128]{2,1,0:T(8,128)S(1)}, f32[8,128,128]{2,1,0:T(8,128)S(1)}, u32[]{:S(2)}, u32[]{:S(2)}) collective-permute-start(f32[8,128,128]{2,1,0:T(8,128)S(1)} %get-tuple-element.31), channel_id=1, source_target_pairs={{0,1},{1,2},{2,3},{3,4},{4,5},{5,6},{6,7},{7,0},{8,9},{9,10},{10,1... | collective-permute-start | bytes 1572872 | tf_op jit(solution)/shard_map/ppermute | solution.py:17
  952.9 16.0 %collective-permute-start.4 = (f32[8,128,128]{2,1,0:T(8,128)S(1)}, f32[8,128,128]{2,1,0:T(8,128)S(1)}, u32[]{:S(2)}, u32[]{:S(2)}) collective-permute-start(f32[8,128,128]{2,1,0:T(8,128)S(1)} %get-tuple-element.26), channel_id=1, source_target_pairs={{0,7},{1,0},{2,1},{3,2},{4,3},{5,4},{6,5},{7,6},{8,15},{9,8},{10,9... | collective-permute-start | bytes 1572872 | tf_op jit(solution)/shard_map/ppermute | solution.py:17
  956.5 15.5 %collective-permute-start.5 = (f32[8,128,128]{2,1,0:T(8,128)S(1)}, f32[8,128,128]{2,1,0:T(8,128)S(1)}, u32[]{:S(2)}, u32[]{:S(2)}) collective-permute-start(f32[8,128,128]{2,1,0:T(8,128)S(1)} %get-tuple-element.27), channel_id=1, source_target_pairs={{0,1},{1,2},{2,3},{3,4},{4,5},{5,6},{6,7},{7,0},{8,9},{9,10},{10,1... | collective-permute-start | bytes 1572872 | tf_op jit(solution)/shard_map/ppermute | solution.py:17
Sparse Core Ops, SparseCore 0:
  375.1 494.8 reduce-scatter.1
where the time goes:
time: 1010 us
  waiting for transfers between devices  502 us (50%)
  local copies, waits for them, and re-layouts  263 us (26%)
  other arithmetic  146 us (14%)
  matrix products  70 us (7%)
  between operations  16.8 us (2%)
    reduce_scatter x1, waiting for transfers between devices, slot_gradient(): lax.psum_scatter(product.reshape(group_rows * lax.axis_size('tok'), block...  489 us
    gather x2, local copies, waits for them, and re-layouts, slot_gradient(): token_tiles = jnp.take(token_blocks, global_ids.reshape(-1), axis=1)  140 us
    select_n x2, other arithmetic, slot_gradient(): token_tiles = jnp.take(token_blocks, global_ids.reshape(-1), axis=1)  75.8 us
    dot_general x1, matrix products, slot_gradient(): jnp.einsum('tacki,tcj->ackij', token_tiles, hidden_cols, preferred_elemen...  70 us
    mul x1, local copies, waits for them, and re-layouts, slot_gradient(): product = product * usable[:, :, :, None, None]  38.3 us
    concatenate x3, local copies, waits for them, and re-layouts, relocate(): jnp.concatenate([head_tile[None], state_now[1:last_slot], tail_tile[None]...  36.6 us
    sub x1, other arithmetic, adam_update(): stepped = weights - learn_rate * (update + weight_decay * weights)  35.4 us
    mul x1, other arithmetic, body(): second_new * keep_mask  27.3 us
  transfers between devices with their start and end apart: 7, of which 5 were waited for; matrix products, arithmetic and copies ran while one was open for 2% of the time, Pallas kernels for 0%

commit v1 on v0

v1 whole, which is shorter than its diff:
```python
import functools

import jax
import jax.numpy as jnp
from jax import lax
from jax.experimental import pallas as pl
from jax.experimental.pallas import tpu as pltpu
from jax.sharding import PartitionSpec as P

beta_one = 0.9
beta_two = 0.95
learn_rate = 0.05
weight_decay = 0.1
adam_eps = 1e-08
adam_steps = 20.0
fix_one = 1.0 - beta_one**adam_steps
fix_two = 1.0 - beta_two**adam_steps

PAIR = 2
CHUNKS = 3


def shifted(value, axis, steps):
    count = lax.axis_size(axis)
    return lax.ppermute(value, axis, [(i, (i + steps) % count) for i in range(count)])


def block_rows(block_mask, columns, first_row, range_rows, capacity):
    window = lax.dynamic_slice_in_dim(block_mask, first_row, range_rows, 0)
    total_cols = block_mask.shape[1]
    selector = (columns[:, None] == jnp.arange(total_cols, dtype=jnp.int32)[None, :]).astype(jnp.int32)
    present = jnp.sum(selector[:, None, :] * window[None, :, :], axis=2)
    local_rows = jnp.arange(range_rows, dtype=jnp.int32)
    upto = (local_rows[None, :] <= local_rows[:, None]).astype(jnp.int32)
    running = jnp.sum(present[:, None, :] * upto[None, :, :], axis=2)
    places = jnp.arange(capacity, dtype=jnp.int32)
    matches = (present[:, None, :] == 1) & (running[:, None, :] == places[None, :, None] + 1)
    row_ids = jnp.sum(jnp.where(matches, local_rows[None, None, :], 0), axis=2)
    return row_ids, jnp.sum(present, axis=1)


def kernel(slot_of, rows_ref, count_ref, mine_ref, other_ref, hidden_ref, w_ref, m_ref, v_ref, *rest):
    ow_ref, om_ref, ov_ref, dense = rest[-4:]
    ranges, half_rows, _ = mine_ref.shape
    capacity, width = w_ref.shape[1], w_ref.shape[3]
    tile = min(512, half_rows)
    for half, lhs_ref in enumerate((mine_ref, other_ref)):

        @pl.loop(0, half_rows // tile)
        def _(step):
            at = pl.multiple_of(step * tile, tile)
            total = jnp.dot(
                lhs_ref[0, pl.ds(at, tile), :], hidden_ref[0], preferred_element_type=jnp.float32
            )
            for t in range(1, ranges):
                total += jnp.dot(
                    lhs_ref[t, pl.ds(at, tile), :], hidden_ref[t], preferred_element_type=jnp.float32
                )
            dense[pl.ds(pl.multiple_of(half * half_rows + at, tile), tile), :] = total

    first_slot = slot_of(pl.program_id(0)) * PAIR
    for s in range(PAIR):
        count = count_ref[first_slot + s]

        @pl.loop(0, capacity)
        def _(j):
            used = j < count

            @pl.when(used)
            def _():
                row = pl.multiple_of(rows_ref[(first_slot + s) * capacity + j] * width, width)
                gradient = dense[pl.ds(row, width), s * width : (s + 1) * width]
                first = beta_one * m_ref[s, j] + (1.0 - beta_one) * gradient
                second = beta_two * v_ref[s, j] + (1.0 - beta_two) * gradient * gradient
                update = (first * (1.0 / fix_one)) / (jnp.sqrt(second * (1.0 / fix_two)) + adam_eps)
                old = w_ref[s, j]
                ow_ref[s, j] = old - learn_rate * (update + weight_decay * old)
                om_ref[s, j] = first
                ov_ref[s, j] = second

            @pl.when(jnp.logical_not(used))
            def _():
                zero = jnp.zeros((width, width), jnp.float32)
                ow_ref[s, j] = zero
                om_ref[s, j] = zero
                ov_ref[s, j] = zero


def run_chunk(pairs, src_of, dst_of, rows, counts, mine, other, hidden, state, previous, total_slots):
    ranges, half_rows, tok_rows = mine.shape
    capacity, width = state[0].shape[1], state[0].shape[3]
    whole = lambda i, *_: (0, 0, 0)
    lhs_spec = pl.BlockSpec(mine.shape, whole, pipeline_mode=pl.Buffered(1))
    block = (PAIR, capacity, width, width)
    state_spec = pl.BlockSpec(block, lambda i, *_: (src_of(i), 0, 0, 0))
    out_spec = pl.BlockSpec(block, lambda i, *_: (dst_of(i), 0, 0, 0))
    out = jax.ShapeDtypeStruct((total_slots,) + block[1:], jnp.float32)
    aliases = {8 + i: i for i in range(3)} if previous else {}
    return pl.pallas_call(
        functools.partial(kernel, dst_of),
        grid_spec=pltpu.PrefetchScalarGridSpec(
            num_scalar_prefetch=2,
            grid=(pairs,),
            in_specs=[lhs_spec, lhs_spec]
            + [pl.BlockSpec((ranges, tok_rows, PAIR * width), lambda i, *_: (0, 0, i))]
            + [state_spec] * 3
            + [pl.BlockSpec(memory_space=pl.ANY)] * len(previous),
            out_specs=[out_spec] * 3,
            scratch_shapes=[pltpu.VMEM((2 * half_rows, PAIR * width), jnp.float32)],
        ),
        out_shape=[out] * 3,
        input_output_aliases=aliases,
        compiler_params=pltpu.CompilerParams(vmem_limit_bytes=44 * 1024 * 1024),
        cost_estimate=pl.CostEstimate(
            flops=4 * pairs * half_rows * ranges * tok_rows * PAIR * width,
            bytes_accessed=pairs * 24 * PAIR * capacity * width * width + 2 * 2 * mine.size,
            transcendentals=0,
        ),
    )(rows, counts, mine, other, hidden, *state, *previous)


def body(features, hidden_grad, block_mask, old_columns, new_columns, weights, first_moment, second_moment):
    ranges, owners = lax.axis_size("tok"), lax.axis_size("blk")
    tok_index, owner_index = lax.axis_index("tok"), lax.axis_index("blk")
    slots, capacity, width = weights.shape[1:4]
    total_rows = block_mask.shape[0]
    range_rows = total_rows // ranges
    tok_rows = features.shape[0]
    last = slots - 1
    state = [x[0] for x in (weights, first_moment, second_moment)]
    pairs = slots // PAIR
    cols = PAIR * width

    def gathered(x):
        return lax.all_gather(x, "tok", axis=0, tiled=False)

    inner = max(pairs - 2, 0)
    bounds = sorted({inner * i // CHUNKS for i in range(CHUNKS + 1)})
    chunks = [(1 + a, 1 + b) for a, b in zip(bounds[:-1], bounds[1:])]
    inner_hidden = [gathered(hidden_grad[:, a * cols : b * cols]) for a, b in chunks]

    core = owner_index % 2
    by_range = features.reshape(tok_rows, ranges, 2, range_rows // 2 * width)
    half = lax.dynamic_index_in_dim(by_range, core, 2, keepdims=False)
    half = jnp.transpose(half, (1, 2, 0))
    mine = lax.all_to_all(half, "tok", 0, 0)
    other = lax.ppermute(mine, "blk", [(i, i ^ 1) for i in range(owners)])

    old_mine = lax.dynamic_index_in_dim(old_columns, owner_index, 0, keepdims=False)
    new_mine = lax.dynamic_index_in_dim(new_columns, owner_index, 0, keepdims=False)
    into_first = new_mine[0] != old_mine[0]
    into_last = new_mine[last] != old_mine[last]
    row_ids, counts = block_rows(block_mask, new_mine, tok_index * range_rows, range_rows, capacity)
    rows = (row_ids + core * (range_rows // 2)) % range_rows
    rows = rows.reshape(-1).astype(jnp.int32)

    ends = [hidden_grad[:, :width], hidden_grad[:, last * width :]]
    lower = [shifted(x, "blk", 1) for x in (ends[0], *(x[0] for x in state))]
    upper = [shifted(x, "blk", -1) for x in (ends[1], *(x[last] for x in state))]
    head = [jnp.where(into_first, u, x) for u, x in zip(upper, (ends[0], *(x[0] for x in state)))]
    tail = [jnp.where(into_last, l, x) for l, x in zip(lower, (ends[1], *(x[last] for x in state)))]
    if pairs > 1:
        h_parts = [head[0], hidden_grad[:, width:cols], hidden_grad[:, (last - 1) * width : last * width], tail[0]]
        s_parts = [
            jnp.concatenate([head[1 + i][None], x[1:PAIR], x[last - 1 : last], tail[1 + i][None]], axis=0)
            for i, x in enumerate(state)
        ]
    else:
        h_parts = [head[0], tail[0]]
        s_parts = [jnp.stack([head[1 + i], tail[1 + i]]) for i in range(3)]
    outer_hidden = gathered(jnp.concatenate(h_parts, axis=1))

    out = []
    for (a, b), hidden in zip(chunks, inner_hidden):
        place = functools.partial(lambda base, i: base + i, a)
        out = run_chunk(b - a, place, place, rows, counts, mine, other, hidden, state, out, slots)
    out = run_chunk(
        min(pairs, 2), lambda i: i, lambda i: i * (pairs - 1), rows, counts, mine, other, outer_hidden, s_parts, out, slots
    )
    return tuple(x[None] for x in out)


def solution(mesh):
    stored = P("tok", "blk", None, None, None)
    return jax.shard_map(
        body,
        mesh=mesh,
        in_specs=(P("tok", None), P("tok", "blk"), P(), P(), P(), stored, stored, stored),
        out_specs=(stored, stored, stored),
        check_vma=False,
    )
```

time: 1010 us -> 269 us (0.27)
  waiting for transfers between devices: 502 us -> 72.9 us
  local copies, waits for them, and re-layouts: 263 us -> 66.8 us
  other arithmetic: 146 us -> 10.8 us
  Pallas kernels: 0 us -> 79.7 us
  matrix products: 70 us -> 0 us
  starting transfers between devices: 9.95 us -> 20.7 us
    reduce_scatter x1 -> x0, waiting for transfers between devices: 489 us -> none  [slot_gradient(): lax.psum_scatter(product.reshape(group_rows * lax.axis_size('tok'), block...]
    gather x14 -> x0, local copies, waits for them, and re-layouts: 148 us -> none  [the longest x2 140 us: slot_gradient(): token_tiles = jnp.take(token_blocks, global_ids.reshape(-1), axis=1)]
    pallas_call x0 -> x4, Pallas kernels: none -> 79.7 us  [run_chunk(): pl.pallas_call(functools.partial(kernel, dst_of), grid_spec=pltpu.Prefetc...]
    select_n x3 -> x2, other arithmetic: 75.8 us -> 1.18 us  [the longest x1 1.17 us: body(): jnp.where(into_first, u, x)]
    dot_general x1 -> x0, matrix products: 70 us -> none  [slot_gradient(): jnp.einsum('tacki,tcj->ackij', token_tiles, hidden_cols, preferred_elemen...]
    all_to_all x0 -> x1, waiting for transfers between devices: none -> 52.9 us  [body(): mine = lax.all_to_all(half, 'tok', 0, 0)]
    mul x1 -> x0, local copies, waits for them, and re-layouts: 38.3 us -> none  [slot_gradient(): product = product * usable[:, :, :, None, None]]
    concatenate x4 -> x0, local copies, waits for them, and re-layouts: 36.6 us -> none  [the longest x3 36.6 us: relocate(): jnp.concatenate([head_tile[None], state_now[1:last_slot], tail_tile[None]...]
  transfers between devices with their start and end apart: 7 -> 14, of which waited for: 5 -> 6; matrix products, arithmetic and copies ran while one was open for 2% -> 26% of each run, Pallas kernels for 0% -> 25%
where the time goes in v1:
time: 269 us; the launch traced here: 267 us
  Pallas kernels  79.7 us (30%)
  waiting for transfers between devices  72.9 us (27%)
  local copies, waits for them, and re-layouts  66.8 us (25%)
  starting transfers between devices  20.7 us (8%)
  between operations  16.5 us (6%)
  other arithmetic  10.8 us (4%)
    pallas_call x4, Pallas kernels, run_chunk(): pl.pallas_call(functools.partial(kernel, dst_of), grid_spec=pltpu.Prefetc...  79.7 us
    all_to_all x1, waiting for transfers between devices, body(): mine = lax.all_to_all(half, 'tok', 0, 0)  52.9 us
    unnamed x19, local copies, waits for them, and re-layouts  24.7 us
    ppermute x8, starting transfers between devices, shifted(): lax.ppermute(value, axis, [(i, (i + steps) % count) for i in range(count)])  15.4 us
    reshape x1, local copies, waits for them, and re-layouts, body(): by_range = features.reshape(tok_rows, ranges, 2, range_rows // 2 * width)  14.6 us
    ppermute x8, waiting for transfers between devices, shifted(): lax.ppermute(value, axis, [(i, (i + steps) % count) for i in range(count)])  12.6 us
    dynamic_slice x1, local copies, waits for them, and re-layouts, body(): half = lax.dynamic_index_in_dim(by_range, core, 2, keepdims=False)  12 us
    squeeze x3, local copies, waits for them, and re-layouts, body(): x[last]  8.51 us
  transfers between devices with their start and end apart: 14, of which 6 were waited for; matrix products, arithmetic and copies ran while one was open for 26% of the time, Pallas kernels for 25%

profile of v1, /device:TPU:0, one launch (start us, length us, event | category | flops | bytes accessed | tf_op | source)
XLA Modules:
  0.0 267.4 jit_solution(8225442360926573224)
XLA Ops:
  7.2 3.6 %fusion.3 = (bf16[512,1024]{1,0:T(8,128)(2,1)}, bf16[512,1024]{1,0:T(8,128)(2,1)}, bf16[512,1024]{1,0:T(8,128)(2,1)}) fusion(bf16[512,3584]{1,0:T(8,128)(2,1)} %param.9), kind=kLoop, calls=%fused_computation.43 | loop fusion | bytes 6291456 | tf_op jit(solution)/shard_map/slice | solution.py:140
  12.4 14.6 %reshape.88 = bf16[512,4,2,1024]{3,2,1,0:T(2,128)(2,1)} reshape(bf16[512,8192]{1,0:T(8,128)(2,1)} %param.8) | data formatting | bytes 16777216 | tf_op jit(solution)/shard_map/reshape | solution.py:143
  27.0 12.0 %constant_dynamic-slice_fusion = bf16[512,4,1,1024]{3,2,1,0:T(2,128)(2,1)} fusion(bf16[512,4,2,1024]{3,2,1,0:T(2,128)(2,1)} %reshape.88, s32[]{:T(128)S(6)} %select_n.79), kind=kLoop, calls=%fused_computation.38 | loop fusion | bytes 8388612 | tf_op jit(solution)/shard_map/jit(dynamic_index_in_dim)/dynamic_slice | solution.py:144
  39.0 19.9 %copy.30 = bf16[512,4,1,1024]{0,3,1,2:T(8,128)(2,1)} copy(bf16[512,4,1,1024]{3,2,1,0:T(2,128)(2,1)} %constant_dynamic-slice_fusion) | data formatting | bytes 8388608
  58.9 5.2 %all-to-all-start = ((bf16[4,1024,512]{2,1,0:T(8,128)(2,1)}), bf16[4,1024,512]{2,1,0:T(8,128)(2,1)}, u32[]{:S(2)}, u32[]{:S(2)}) async-start(bf16[4,1024,512]{2,1,0:T(8,128)(2,1)} %bitcast.77), calls=%async_computation | async-start | bytes 8388608 | tf_op jit(solution)/shard_map/all_to_all | solution.py:146
  64.2 2.7 slice_bitcast_fusion.11
  66.8 4.2 %collective-permute-start.3 = (f32[8,128,128]{2,1,0:T(8,128)}, f32[8,128,128]{2,1,0:T(8,128)S(1)}, u32[]{:S(2)}, u32[]{:S(2)}) collective-permute-start(f32[8,128,128]{2,1,0:T(8,128)} %get-tuple-element.43), channel_id=1, source_target_pairs={{0,7},{1,0},{2,1},{3,2},{4,3},{5,4},{6,5},{7,6},{8,15},{9,8},{10,9... | collective-permute-start | bytes 1572872 | tf_op jit(solution)/shard_map/ppermute | solution.py:25
  71.0 52.9 %all-to-all-done.mine_ref = bf16[4,1024,512]{2,1,0:T(8,128)(2,1)} async-done(((bf16[4,1024,512]{2,1,0:T(8,128)(2,1)}), bf16[4,1024,512]{2,1,0:T(8,128)(2,1)}, u32[]{:S(2)}, u32[]{:S(2)}) %all-to-all-start) | async-done | bytes 4194336 | tf_op jit(solution)/shard_map/all_to_all | solution.py:146
  124.9 4.0 %collective-permute-start.1 = (bf16[512,128]{1,0:T(8,128)(2,1)S(1)}, bf16[512,128]{1,0:T(8,128)(2,1)S(1)}, u32[]{:S(2)}, u32[]{:S(2)}) collective-permute-start(bf16[512,128]{1,0:T(8,128)(2,1)S(1)} %get-tuple-element.54), channel_id=1, source_target_pairs={{0,7},{1,0},{2,1},{3,2},{4,3},{5,4},{6,5},{7,6},{8,15},{9,8},{10,9... | collective-permute-start | bytes 393224 | tf_op jit(solution)/shard_map/ppermute | solution.py:25
  135.2 2.9 %slice_bitcast_fusion.7 = (f32[8,128,128]{2,1,0:T(8,128)}, f32[1,8,128,128]{3,2,1,0:T(8,128)}, f32[8,128,128]{2,1,0:T(8,128)}, f32[1,8,128,128]{3,2,1,0:T(8,128)}) fusion(f32[1,28,8,128,128]{4,3,2,1,0:T(8,128)} %param.14), kind=kLoop, calls=%fused_computation.17 | loop fusion | bytes 4194304 | tf_op jit(solution)/shard_map/squeeze | solution.py:159
  138.1 2.9 %slice_bitcast_fusion.3 = (f32[8,128,128]{2,1,0:T(8,128)}, f32[1,8,128,128]{3,2,1,0:T(8,128)}, f32[8,128,128]{2,1,0:T(8,128)}, f32[1,8,128,128]{3,2,1,0:T(8,128)}) fusion(f32[1,28,8,128,128]{4,3,2,1,0:T(8,128)} %param.15), kind=kLoop, calls=%fused_computation.11 | loop fusion | bytes 4194304 | tf_op jit(solution)/shard_map/squeeze | solution.py:159
  141.1 3.6 %collective-permute-start.5 = (f32[8,128,128]{2,1,0:T(8,128)}, f32[8,128,128]{2,1,0:T(8,128)S(1)}, u32[]{:S(2)}, u32[]{:S(2)}) collective-permute-start(f32[8,128,128]{2,1,0:T(8,128)} %get-tuple-element.37), channel_id=1, source_target_pairs={{0,7},{1,0},{2,1},{3,2},{4,3},{5,4},{6,5},{7,6},{8,15},{9,8},{10,9... | collective-permute-start | bytes 1572872 | tf_op jit(solution)/shard_map/ppermute | solution.py:25
  146.7 3.6 %collective-permute-start.7 = (f32[8,128,128]{2,1,0:T(8,128)}, f32[8,128,128]{2,1,0:T(8,128)S(1)}, u32[]{:S(2)}, u32[]{:S(2)}) collective-permute-start(f32[8,128,128]{2,1,0:T(8,128)} %get-tuple-element.31), channel_id=1, source_target_pairs={{0,7},{1,0},{2,1},{3,2},{4,3},{5,4},{6,5},{7,6},{8,15},{9,8},{10,9... | collective-permute-start | bytes 1572872 | tf_op jit(solution)/shard_map/ppermute | solution.py:25
  151.7 5.6 %collective-permute-done.5 = f32[8,128,128]{2,1,0:T(8,128)S(1)} collective-permute-done((f32[8,128,128]{2,1,0:T(8,128)}, f32[8,128,128]{2,1,0:T(8,128)S(1)}, u32[]{:S(2)}, u32[]{:S(2)}) %collective-permute-start.5) | collective-permute-done | bytes 524320 | tf_op jit(solution)/shard_map/ppermute | solution.py:25
  157.4 3.6 %collective-permute-done.6 = f32[8,128,128]{2,1,0:T(8,128)S(1)} collective-permute-done((f32[8,128,128]{2,1,0:T(8,128)}, f32[8,128,128]{2,1,0:T(8,128)S(1)}, u32[]{:S(2)}, u32[]{:S(2)}) %collective-permute-start.6) | collective-permute-done | bytes 524320 | tf_op jit(solution)/shard_map/ppermute | solution.py:25
  164.8 2.7 %collective-permute-done.8 = f32[8,128,128]{2,1,0:T(8,128)S(1)} collective-permute-done((f32[8,128,128]{2,1,0:T(8,128)}, f32[8,128,128]{2,1,0:T(8,128)S(1)}, u32[]{:S(2)}, u32[]{:S(2)}) %collective-permute-start.8) | collective-permute-done | bytes 524320 | tf_op jit(solution)/shard_map/ppermute | solution.py:25
  170.4 22.5 %shard_map.103 = (f32[28,8,128,128]{3,2,1,0:T(8,128)}, f32[28,8,128,128]{3,2,1,0:T(8,128)}, f32[28,8,128,128]{3,2,1,0:T(8,128)}) custom-call(s32[224]{0:T(256)S(1)} %and_select_fusion.rows_ref, s32[28]{0:T(128)S(1)} %get-tuple-element.27.count_ref, bf16[4,1024,512]{2,1,0:T(8,128)(2,1)} %all-to-all-done.mine_ref, ...), custom_call_target="tpu_custom_call" | custom-call | flops 8589934592 | bytes 33554432 | tf_op jit(solution)/shard_map/pallas_call | solution.py:99
  193.0 22.2 %shard_map.104 = (f32[28,8,128,128]{3,2,1,0:T(8,128)}, f32[28,8,128,128]{3,2,1,0:T(8,128)}, f32[28,8,128,128]{3,2,1,0:T(8,128)}) custom-call(s32[224]{0:T(256)S(1)} %and_select_fusion.rows_ref, s32[28]{0:T(128)S(1)} %get-tuple-element.27.count_ref, ...), custom_call_target="tpu_custom_call", output_to_operand_aliasing={{0}: (8, {}), {1}: (9, {}), {2}: (10, {})} | custom-call | flops 8589934592 | bytes 33554432 | tf_op jit(solution)/shard_map/pallas_call | solution.py:99
  215.1 21.9 %shard_map.105 = (f32[28,8,128,128]{3,2,1,0:T(8,128)}, f32[28,8,128,128]{3,2,1,0:T(8,128)}, f32[28,8,128,128]{3,2,1,0:T(8,128)}) custom-call(s32[224]{0:T(256)S(1)} %and_select_fusion.rows_ref, s32[28]{0:T(128)S(1)} %get-tuple-element.27.count_ref, ...), custom_call_target="tpu_custom_call", output_to_operand_aliasing={{0}: (8, {}), {1}: (9, {}), {2}: (10, {})} | custom-call | flops 8589934592 | bytes 33554432 | tf_op jit(solution)/shard_map/pallas_call | solution.py:99
  237.0 6.0 %all-gather.9.cloned.1.call-done = bf16[2048,512]{1,0:T(8,128)(2,1)} async-done(((bf16[512,512]{1,0:T(8,128)(2,1)}), bf16[2048,512]{1,0:T(8,128)(2,1)}) %all-gather.9.cloned.1.call-update) | async-done | bytes 2097168 | tf_op jit(solution)/shard_map/all_gather | solution.py:135
  243.0 1.6 copy-done.2
  244.6 1.6 copy-done.3
  246.2 1.6 copy-done.4
  247.8 13.1 %shard_map.106 = (f32[28,8,128,128]{3,2,1,0:T(8,128)}, f32[28,8,128,128]{3,2,1,0:T(8,128)}, f32[28,8,128,128]{3,2,1,0:T(8,128)}) custom-call(s32[224]{0:T(256)S(1)} %and_select_fusion.rows_ref, s32[28]{0:T(128)S(1)} %get-tuple-element.27.count_ref, ...), custom_call_target="tpu_custom_call", output_to_operand_aliasing={{0}: (8, {}), {1}: (9, {}), {2}: (10, {})} | custom-call | flops 4294967296 | bytes 20971520 | tf_op jit(solution)/shard_map/pallas_call | solution.py:99
  (62 shorter events, 16.3 us)
Async XLA Ops:
  7.2 122.5 %copy-start = (s32[64,224]{1,0:T(8,128)S(1)}, s32[64,224]{1,0:T(8,128)}, u32[]{:S(2)}) copy-start(s32[64,224]{1,0:T(8,128)} %param.10) | copy-start | bytes 172036
  7.2 163.2 %all-gather.15.cloned.1.call-start = ((), (), s32[]{:S(2)}) async-start(), calls=%async_computation.4 | async-start | bytes 5242880 | tf_op jit(solution)/shard_map/all_gather | solution.py:135
  10.9 182.1 %all-gather.13.cloned.1.call-start = ((), (), s32[]{:S(2)}) async-start(), calls=%async_computation.3 | async-start | bytes 5242880 | tf_op jit(solution)/shard_map/all_gather | solution.py:135
  11.7 203.5 %all-gather.11.cloned.1.call-start = ((), (), s32[]{:S(2)}) async-start(), calls=%async_computation.2 | async-start | bytes 5242880 | tf_op jit(solution)/shard_map/all_gather | solution.py:135
  58.9 65.0 %all-to-all-start = ((bf16[4,1024,512]{2,1,0:T(8,128)(2,1)}), bf16[4,1024,512]{2,1,0:T(8,128)(2,1)}, u32[]{:S(2)}, u32[]{:S(2)}) async-start(bf16[4,1024,512]{2,1,0:T(8,128)(2,1)} %bitcast.77), calls=%async_computation | async-start | bytes 8388608 | tf_op jit(solution)/shard_map/all_to_all | solution.py:146
  64.2 178.9 %all-gather.9.cloned.1.call-start = ((), (), s32[]{:S(2)}) async-start(), calls=%async_computation.1 | async-start | bytes 2621440 | tf_op jit(solution)/shard_map/all_gather | solution.py:135
  66.8 79.9 %collective-permute-start.3 = (f32[8,128,128]{2,1,0:T(8,128)}, f32[8,128,128]{2,1,0:T(8,128)S(1)}, u32[]{:S(2)}, u32[]{:S(2)}) collective-permute-start(f32[8,128,128]{2,1,0:T(8,128)} %get-tuple-element.43), channel_id=1, source_target_pairs={{0,7},{1,0},{2,1},{3,2},{4,3},{5,4},{6,5},{7,6},{8,15},{9,8},{10,9... | collective-permute-start | bytes 1572872 | tf_op jit(solution)/shard_map/ppermute | solution.py:25
  71.0 79.3 %collective-permute-start.4 = (f32[8,128,128]{2,1,0:T(8,128)}, f32[8,128,128]{2,1,0:T(8,128)S(1)}, u32[]{:S(2)}, u32[]{:S(2)}) collective-permute-start(f32[8,128,128]{2,1,0:T(8,128)} %get-tuple-element.45), channel_id=1, source_target_pairs={{0,1},{1,2},{2,3},{3,4},{4,5},{5,6},{6,7},{7,0},{8,9},{9,10},{10,1... | collective-permute-start | bytes 1572872 | tf_op jit(solution)/shard_map/ppermute | solution.py:25
  123.9 46.5 %collective-permute-start = (bf16[4,1024,512]{2,1,0:T(8,128)(2,1)}, bf16[4,1024,512]{2,1,0:T(8,128)(2,1)}, u32[]{:S(2)}, u32[]{:S(2)}) collective-permute-start(bf16[4,1024,512]{2,1,0:T(8,128)(2,1)} %all-to-all-done.mine_ref), channel_id=1, source_target_pairs={{0,1},{1,0},{2,3},{3,2},{4,5},{5,4},{6,7},{7,6},{8,9},{9,8},{10,11... | collective-permute-start | bytes 12582920 | tf_op jit(solution)/shard_map/ppermute | solution.py:147
  124.9 16.1 %collective-permute-start.1 = (bf16[512,128]{1,0:T(8,128)(2,1)S(1)}, bf16[512,128]{1,0:T(8,128)(2,1)S(1)}, u32[]{:S(2)}, u32[]{:S(2)}) collective-permute-start(bf16[512,128]{1,0:T(8,128)(2,1)S(1)} %get-tuple-element.54), channel_id=1, source_target_pairs={{0,7},{1,0},{2,1},{3,2},{4,3},{5,4},{6,5},{7,6},{8,15},{9,8},{10,9... | collective-permute-start | bytes 393224 | tf_op jit(solution)/shard_map/ppermute | solution.py:25
  128.9 15.7 %collective-permute-start.2 = (bf16[512,128]{1,0:T(8,128)(2,1)S(1)}, bf16[512,128]{1,0:T(8,128)(2,1)S(1)}, u32[]{:S(2)}, u32[]{:S(2)}) collective-permute-start(bf16[512,128]{1,0:T(8,128)(2,1)S(1)} %get-tuple-element.55), channel_id=1, source_target_pairs={{0,1},{1,2},{2,3},{3,4},{4,5},{5,6},{6,7},{7,0},{8,9},{9,10},{10,1... | collective-permute-start | bytes 393224 | tf_op jit(solution)/shard_map/ppermute | solution.py:25
  141.1 16.3 %collective-permute-start.5 = (f32[8,128,128]{2,1,0:T(8,128)}, f32[8,128,128]{2,1,0:T(8,128)S(1)}, u32[]{:S(2)}, u32[]{:S(2)}) collective-permute-start(f32[8,128,128]{2,1,0:T(8,128)} %get-tuple-element.37), channel_id=1, source_target_pairs={{0,7},{1,0},{2,1},{3,2},{4,3},{5,4},{6,5},{7,6},{8,15},{9,8},{10,9... | collective-permute-start | bytes 1572872 | tf_op jit(solution)/shard_map/ppermute | solution.py:25
  144.7 16.3 %collective-permute-start.6 = (f32[8,128,128]{2,1,0:T(8,128)}, f32[8,128,128]{2,1,0:T(8,128)S(1)}, u32[]{:S(2)}, u32[]{:S(2)}) collective-permute-start(f32[8,128,128]{2,1,0:T(8,128)} %get-tuple-element.39), channel_id=1, source_target_pairs={{0,1},{1,2},{2,3},{3,4},{4,5},{5,6},{6,7},{7,0},{8,9},{9,10},{10,1... | collective-permute-start | bytes 1572872 | tf_op jit(solution)/shard_map/ppermute | solution.py:25
  146.7 18.1 %collective-permute-start.7 = (f32[8,128,128]{2,1,0:T(8,128)}, f32[8,128,128]{2,1,0:T(8,128)S(1)}, u32[]{:S(2)}, u32[]{:S(2)}) collective-permute-start(f32[8,128,128]{2,1,0:T(8,128)} %get-tuple-element.31), channel_id=1, source_target_pairs={{0,7},{1,0},{2,1},{3,2},{4,3},{5,4},{6,5},{7,6},{8,15},{9,8},{10,9... | collective-permute-start | bytes 1572872 | tf_op jit(solution)/shard_map/ppermute | solution.py:25
  150.3 17.2 %collective-permute-start.8 = (f32[8,128,128]{2,1,0:T(8,128)}, f32[8,128,128]{2,1,0:T(8,128)S(1)}, u32[]{:S(2)}, u32[]{:S(2)}) collective-permute-start(f32[8,128,128]{2,1,0:T(8,128)} %get-tuple-element.33), channel_id=1, source_target_pairs={{0,1},{1,2},{2,3},{3,4},{4,5},{5,6},{6,7},{7,0},{8,9},{9,10},{10,1... | collective-permute-start | bytes 1572872 | tf_op jit(solution)/shard_map/ppermute | solution.py:25
  151.7 10.9 %copy-start.7 = (f32[1,8,128,128]{3,2,1,0:T(8,128)S(1)}, f32[1,8,128,128]{3,2,1,0:T(8,128)}, u32[]{:S(2)}) copy-start(f32[1,8,128,128]{3,2,1,0:T(8,128)} %get-tuple-element.38) | copy-start | bytes 1572868
  151.7 10.9 %copy-start.8 = (f32[1,8,128,128]{3,2,1,0:T(8,128)S(1)}, f32[1,8,128,128]{3,2,1,0:T(8,128)}, u32[]{:S(2)}) copy-start(f32[1,8,128,128]{3,2,1,0:T(8,128)} %get-tuple-element.40) | copy-start | bytes 1572868
  162.6 6.3 %copy-start.5 = (f32[1,8,128,128]{3,2,1,0:T(8,128)S(1)}, f32[1,8,128,128]{3,2,1,0:T(8,128)}, u32[]{:S(2)}) copy-start(f32[1,8,128,128]{3,2,1,0:T(8,128)} %get-tuple-element.32) | copy-start | bytes 1572868
  162.6 6.3 %copy-start.6 = (f32[1,8,128,128]{3,2,1,0:T(8,128)S(1)}, f32[1,8,128,128]{3,2,1,0:T(8,128)}, u32[]{:S(2)}) copy-start(f32[1,8,128,128]{3,2,1,0:T(8,128)} %get-tuple-element.34) | copy-start | bytes 1572868
  243.0 1.6 copy-start.2
  244.6 1.6 copy-start.3
  246.2 1.6 copy-start.4
  247.8 13.1 %copy-start.1 = (s32[64,224]{1,0:T(8,128)S(1)}, s32[64,224]{1,0:T(8,128)}, u32[]{:S(2)}) copy-start(s32[64,224]{1,0:T(8,128)} %param.10) | copy-start | bytes 172036
Sparse Core Ops, SparseCore 0:
  11.0 55.4 all-gather.14
  68.3 82.9 all-gather.12
  153.2 52.7 all-gather.10
  207.7 35.3 all-gather.8

commit v2 on v1

v2 whole, which is shorter than its diff:
```python
import functools

import jax
import jax.numpy as jnp
from jax import lax
from jax.experimental import pallas as pl
from jax.experimental.pallas import tpu as pltpu
from jax.sharding import PartitionSpec as P

beta_one = 0.9
beta_two = 0.95
learn_rate = 0.05
weight_decay = 0.1
adam_eps = 1e-08
adam_steps = 20.0
fix_one = 1.0 - beta_one**adam_steps
fix_two = 1.0 - beta_two**adam_steps

PAIR = 2
INNER = ((6, False), (6, False))
OUTER_GATHER = False
OUTER_AT = 2


def shifted(value, axis, steps):
    count = lax.axis_size(axis)
    return lax.ppermute(value, axis, [(i, (i + steps) % count) for i in range(count)])


def block_rows(block_mask, columns, first_row, range_rows, capacity):
    window = lax.dynamic_slice_in_dim(block_mask, first_row, range_rows, 0)
    total_cols = block_mask.shape[1]
    selector = (columns[:, None] == jnp.arange(total_cols, dtype=jnp.int32)[None, :]).astype(jnp.int32)
    present = jnp.sum(selector[:, None, :] * window[None, :, :], axis=2)
    local_rows = jnp.arange(range_rows, dtype=jnp.int32)
    upto = (local_rows[None, :] <= local_rows[:, None]).astype(jnp.int32)
    running = jnp.sum(present[:, None, :] * upto[None, :, :], axis=2)
    places = jnp.arange(capacity, dtype=jnp.int32)
    matches = (present[:, None, :] == 1) & (running[:, None, :] == places[None, :, None] + 1)
    row_ids = jnp.sum(jnp.where(matches, local_rows[None, None, :], 0), axis=2)
    return row_ids, jnp.sum(present, axis=1)


def swapped(value, axis, distance):
    count = lax.axis_size(axis)
    return lax.ppermute(value, axis, [(i, i ^ distance) for i in range(count)])


def kernel(slot_of, ranges, terms, rows_ref, count_ref, *refs):
    mine, other = refs[:ranges], refs[ranges : 2 * ranges]
    sources = 1 + max(source for source, _, _, _ in terms)
    hidden = refs[2 * ranges : 2 * ranges + sources]
    w_ref, m_ref, v_ref = refs[2 * ranges + sources : 2 * ranges + sources + 3]
    ow_ref, om_ref, ov_ref, dense = refs[-4:]
    half_rows = mine[0].shape[0]
    capacity, width = w_ref.shape[1], w_ref.shape[3]
    tile = min(512, half_rows)
    me = count_ref[count_ref.shape[0] - 1]
    for half, lhs in enumerate((mine, other)):

        @pl.loop(0, half_rows // tile)
        def _(step):
            at = pl.multiple_of(step * tile, tile)
            total = None
            for source, d, low, high in terms:
                ref = hidden[source]
                rhs = ref[me ^ d] if len(ref.shape) == 3 else ref[...]
                part = jnp.dot(
                    lhs[d][pl.ds(at, tile), low:high], rhs, preferred_element_type=jnp.float32
                )
                total = part if total is None else total + part
            dense[pl.ds(pl.multiple_of(half * half_rows + at, tile), tile), :] = total

    first_slot = slot_of(pl.program_id(0)) * PAIR
    for s in range(PAIR):
        count = count_ref[first_slot + s]

        @pl.loop(0, capacity)
        def _(j):
            used = j < count

            @pl.when(used)
            def _():
                row = pl.multiple_of(rows_ref[(first_slot + s) * capacity + j] * width, width)
                gradient = dense[pl.ds(row, width), s * width : (s + 1) * width]
                first = beta_one * m_ref[s, j] + (1.0 - beta_one) * gradient
                second = beta_two * v_ref[s, j] + (1.0 - beta_two) * gradient * gradient
                update = (first * (1.0 / fix_one)) / (jnp.sqrt(second * (1.0 / fix_two)) + adam_eps)
                old = w_ref[s, j]
                ow_ref[s, j] = old - learn_rate * (update + weight_decay * old)
                om_ref[s, j] = first
                ov_ref[s, j] = second

            @pl.when(jnp.logical_not(used))
            def _():
                zero = jnp.zeros((width, width), jnp.float32)
                ow_ref[s, j] = zero
                om_ref[s, j] = zero
                ov_ref[s, j] = zero


def run_chunk(pairs, src_of, dst_of, rows, counts, lhs, hidden, state, previous, total_slots):
    ranges = len(lhs) // 2
    half_rows, tok_rows = lhs[0].shape
    capacity, width = state[0].shape[1], state[0].shape[3]
    terms, hidden_arrays, hidden_at = hidden
    lhs_specs = [pl.BlockSpec(x.shape, lambda i, *_: (0, 0), pipeline_mode=pl.Buffered(1)) for x in lhs]
    hidden_specs = []
    for x, at in zip(hidden_arrays, hidden_at):
        if x.ndim == 3:
            hidden_specs.append(pl.BlockSpec(x.shape[:2] + (PAIR * width,), lambda i, *_, at=at: (0, 0, at + i)))
        else:
            hidden_specs.append(pl.BlockSpec((x.shape[0], PAIR * width), lambda i, *_, at=at: (0, at + i)))
    block = (PAIR, capacity, width, width)
    state_spec = pl.BlockSpec(block, lambda i, *_: (src_of(i), 0, 0, 0))
    out_spec = pl.BlockSpec(block, lambda i, *_: (dst_of(i), 0, 0, 0))
    out = jax.ShapeDtypeStruct((total_slots,) + block[1:], jnp.float32)
    first_alias = 2 + len(lhs) + len(hidden_arrays) + 3
    return pl.pallas_call(
        functools.partial(kernel, dst_of, ranges, terms),
        grid_spec=pltpu.PrefetchScalarGridSpec(
            num_scalar_prefetch=2,
            grid=(pairs,),
            in_specs=lhs_specs + hidden_specs + [state_spec] * 3
            + [pl.BlockSpec(memory_space=pl.ANY)] * len(previous),
            out_specs=[out_spec] * 3,
            scratch_shapes=[pltpu.VMEM((2 * half_rows, PAIR * width), jnp.float32)],
        ),
        out_shape=[out] * 3,
        input_output_aliases={first_alias + i: i for i in range(len(previous))},
        compiler_params=pltpu.CompilerParams(vmem_limit_bytes=44 * 1024 * 1024),
        cost_estimate=pl.CostEstimate(
            flops=8 * pairs * half_rows * ranges * tok_rows * PAIR * width,
            bytes_accessed=pairs * 24 * PAIR * capacity * width * width + 4 * ranges * lhs[0].size,
            transcendentals=0,
        ),
    )(rows, counts, *lhs, *hidden_arrays, *state, *previous)


def behind(value, earlier):
    return lax.optimization_barrier((value, earlier))[0]


def everywhere(own, own_at, sent, gather, landed):
    ranges = lax.axis_size("tok")
    tokens = sent.shape[0]
    if gather:
        whole = lax.all_gather(sent, "tok", axis=0, tiled=False)
        return [(0, d, 0, tokens) for d in range(ranges)], [whole], [0]
    terms, arrays = [(0, 0, 0, tokens)], [own]
    if ranges == 4:
        one, two = swapped(sent, "tok", 1), swapped(sent, "tok", 2)
        landed.append((one, two))
        cut = tokens // 2
        low, high = swapped(two[:cut], "tok", 1), swapped(one[cut:], "tok", 2)
        arrays += [one, two, low, high]
        terms += [(1, 1, 0, tokens), (2, 2, 0, tokens), (3, 3, 0, cut), (4, 3, cut, tokens)]
    else:
        for d in range(1, ranges):
            arrays.append(swapped(sent, "tok", d))
            terms.append((d, d, 0, tokens))
    return terms, arrays, [own_at] + [0] * (len(arrays) - 1)


def body(features, hidden_grad, block_mask, old_columns, new_columns, weights, first_moment, second_moment):
    ranges = lax.axis_size("tok")
    tok_index, owner_index = lax.axis_index("tok"), lax.axis_index("blk")
    slots, capacity, width = weights.shape[1:4]
    range_rows = block_mask.shape[0] // ranges
    last = slots - 1
    state = [x[0] for x in (weights, first_moment, second_moment)]
    pairs = slots // PAIR
    cols = PAIR * width

    inner = max(pairs - 2, 0)
    shares = sum(n for n, _ in INNER)
    chunks, done, seen = [], 0, 0
    for share, gather in INNER:
        seen += share
        until = inner * seen // shares
        if until > done:
            chunks.append((1 + done, 1 + until, gather))
        done = until
    core = owner_index % 2
    half_cols = range_rows // 2 * width

    def rows_of(range_index, half):
        start = (range_index * 2 + half) * half_cols
        return lax.dynamic_slice_in_dim(features, start, half_cols, 1).T

    going = [rows_of(tok_index ^ d, core) for d in range(1, ranges)]
    mine = [rows_of(tok_index, core)] + [swapped(x, "tok", d + 1) for d, x in enumerate(going)]
    other = [rows_of(tok_index, 1 - core)] + [swapped(x, "blk", 1) for x in mine[1:]]
    lhs = mine + other

    landed = [going, mine[1:]]

    def sent_columns(own, own_at, sent, gather):
        sent = behind(sent, landed[-2])
        return everywhere(own, own_at, sent, gather, landed)

    inner_parts = [
        sent_columns(hidden_grad, a, hidden_grad[:, a * cols : b * cols], gather) for a, b, gather in chunks
    ]

    old_mine = lax.dynamic_index_in_dim(old_columns, owner_index, 0, keepdims=False)
    new_mine = lax.dynamic_index_in_dim(new_columns, owner_index, 0, keepdims=False)
    into_first = new_mine[0] != old_mine[0]
    into_last = new_mine[last] != old_mine[last]
    row_ids, counts = block_rows(block_mask, new_mine, tok_index * range_rows, range_rows, capacity)
    rows = (row_ids + core * (range_rows // 2)) % range_rows
    rows = rows.reshape(-1).astype(jnp.int32)
    counts = jnp.concatenate([counts, tok_index[None]]).astype(jnp.int32)

    h_first, h_last = hidden_grad[:, :width], hidden_grad[:, last * width :]
    s_first, s_last = jnp.stack([x[0] for x in state]), jnp.stack([x[last] for x in state])
    h_head = jnp.where(into_first, shifted(h_last, "blk", -1), h_first)
    h_tail = jnp.where(into_last, shifted(h_first, "blk", 1), h_last)
    s_head = jnp.where(into_first, shifted(s_last, "blk", -1), s_first)
    s_tail = jnp.where(into_last, shifted(s_first, "blk", 1), s_last)
    if pairs > 1:
        h_parts = [h_head, hidden_grad[:, width:cols], hidden_grad[:, (last - 1) * width : last * width], h_tail]
        s_outer = [
            jnp.concatenate([s_head[i][None], x[1:PAIR], x[last - 1 : last], s_tail[i][None]], axis=0)
            for i, x in enumerate(state)
        ]
    else:
        h_parts = [h_head, h_tail]
        s_outer = [jnp.stack([s_head[i], s_tail[i]]) for i in range(3)]
    h_outer = jnp.concatenate(h_parts, axis=1)
    outer_part = sent_columns(h_outer, 0, h_outer, OUTER_GATHER)

    jobs = []
    for (a, b, _), part in zip(chunks, inner_parts):
        place = functools.partial(lambda base, i: base + i, a)
        jobs.append((b - a, place, place, part, state))
    outer = (min(pairs, 2), lambda i: i, lambda i: i * (pairs - 1), outer_part, s_outer)
    jobs.insert(OUTER_AT, outer)
    out = []
    for count, src_of, dst_of, part, held in jobs:
        out = run_chunk(count, src_of, dst_of, rows, counts, lhs, part, held, out, slots)
    return tuple(x[None] for x in out)


def solution(mesh):
    stored = P("tok", "blk", None, None, None)
    return jax.shard_map(
        body,
        mesh=mesh,
        in_specs=(P("tok", None), P("tok", "blk"), P(), P(), P(), stored, stored, stored),
        out_specs=(stored, stored, stored),
        check_vma=False,
    )
```

time: 269 us -> 225 us (0.84)
  local copies, waits for them, and re-layouts: 66.8 us -> 33.2 us
  between operations: 16.5 us -> 3.36 us
  Pallas kernels: 79.7 us -> 71 us
  waiting for transfers between devices: 72.9 us -> 79.9 us
  starting transfers between devices: 20.7 us -> 25.3 us
    ppermute x1 -> x18, waiting for transfers between devices: 0.01 us -> 75.9 us  [swapped(): return lax.ppermute(value, axis, [(i, i ^ distance) for i in range(count)])]
    all_to_all x1 -> x0, waiting for transfers between devices: 52.9 us -> none  [body(): mine = lax.all_to_all(half, 'tok', 0, 0)]
    ppermute x1 -> x18, starting transfers between devices: 0.01 us -> 21.5 us  [swapped(): return lax.ppermute(value, axis, [(i, i ^ distance) for i in range(count)])]
    reshape x1 -> x0, local copies, waits for them, and re-layouts: 14.6 us -> none  [body(): by_range = features.reshape(tok_rows, ranges, 2, range_rows // 2 * width)]
    unnamed x19 -> x51, local copies, waits for them, and re-layouts: 24.7 us -> 10.5 us
    ppermute x8 -> x4, starting transfers between devices: 15.4 us -> 3.83 us  [shifted(): lax.ppermute(value, axis, [(i, (i + steps) % count) for i in range(count)])]
    slice x1 -> x11, local copies, waits for them, and re-layouts: 0.99 us -> 12.4 us  [the longest x2 6.79 us: body(): x[1:PAIR]]
    pallas_call x4 -> x3, Pallas kernels: 79.7 us -> 71 us  [run_chunk(): pl.pallas_call(functools.partial(kernel, dst_of, ranges, terms), grid_spe...]
  transfers between devices with their start and end apart: 14 -> 22, of which waited for: 6 -> 9; matrix products, arithmetic and copies ran while one was open for 26% -> 13% of each run, Pallas kernels for 25% -> 26%
where the time goes in v2:
time: 225 us
  waiting for transfers between devices  79.9 us (36%)
  Pallas kernels  71 us (32%)
  local copies, waits for them, and re-layouts  33.2 us (15%)
  starting transfers between devices  25.3 us (11%)
  other arithmetic  12.2 us (5%)
  between operations  3.36 us (1%)
    ppermute x18, waiting for transfers between devices, swapped(): return lax.ppermute(value, axis, [(i, i ^ distance) for i in range(count)])  75.9 us
    pallas_call x3, Pallas kernels, run_chunk(): pl.pallas_call(functools.partial(kernel, dst_of, ranges, terms), grid_spe...  71 us
    ppermute x18, starting transfers between devices, swapped(): return lax.ppermute(value, axis, [(i, i ^ distance) for i in range(count)])  21.5 us
    unnamed x51, local copies, waits for them, and re-layouts  10.5 us
    slice x2, local copies, waits for them, and re-layouts, body(): x[1:PAIR]  6.79 us
    dynamic_slice x1, local copies, waits for them, and re-layouts, rows_of(): return lax.dynamic_slice_in_dim(features, start, half_cols, 1).T  4.82 us
    concatenate x3, other arithmetic, body(): jnp.concatenate([s_head[i][None], x[1:PAIR], x[last - 1:last], s_tail[i][...  4.68 us
  transfers between devices with their start and end apart: 22, of which 9 were waited for; matrix products, arithmetic and copies ran while one was open for 13% of the time, Pallas kernels for 26%

profile of v2, /device:TPU:0, one launch (start us, length us, event | category | flops | bytes accessed | tf_op | source)
XLA Modules:
  0.0 224.9 jit_solution(2465521796706133537)
XLA Ops:
  0.7 4.8 %constant_dynamic-slice_fusion.1 = (bf16[512,1024]{1,0:T(8,128)(2,1)}, bf16[512,1024]{1,0:T(8,128)(2,1)S(1)}, bf16[512,1024]{1,0:T(8,128)(2,1)S(1)}, bf16[512,1024]{1,0:T(8,128)(2,1)S(1)}, bf16[512,1024]{1,0:T(8,128)(2,1)}) fusion(bf16[512,8192]{1,0:T(8,128)(2,1)} %param.8, s32[]{:T(128)S(6)} %select_n.78, s32[]{:T(128)S(6)} %select_n.77, s32[]{:T(128)S(6)} %select_n.76, ...), kind=kLoop, calls=%fused_computation.35 | loop fusion | bytes 10485780 | tf_op jit(solution)/shard_map/dynamic_slice | solution.py:189
  9.5 3.2 %fusion.3 = (bf16[512,1536]{1,0:T(8,128)(2,1)}, bf16[512,1536]{1,0:T(8,128)(2,1)S(1)}) fusion(bf16[512,3584]{1,0:T(8,128)(2,1)} %refs_8_.3), kind=kLoop, calls=%fused_computation.46 | loop fusion | bytes 6291456 | tf_op jit(solution)/shard_map/slice | solution.py:203
  12.8 2.9 %collective-permute-start.9 = (bf16[512,1536]{1,0:T(8,128)(2,1)S(1)}, bf16[512,1536]{1,0:T(8,128)(2,1)}, u32[]{:S(2)}, u32[]{:S(2)}) collective-permute-start(bf16[512,1536]{1,0:T(8,128)(2,1)S(1)} %get-tuple-element.15), channel_id=1, source_target_pairs={{0,16},{8,24},{16,0},{24,8},{1,17},{9,25},{17,1},{25,9},{2,18},{10... | collective-permute-start | bytes 4718600 | tf_op jit(solution)/shard_map/ppermute | solution.py:46
  18.7 2.2 collective-permute-start.6
  20.9 2.7 %slice_bitcast_fusion.5 = (f32[1,8,128,128]{3,2,1,0:T(8,128)}, f32[1,8,128,128]{3,2,1,0:T(8,128)}, f32[1,8,128,128]{3,2,1,0:T(8,128)S(1)}, f32[1,8,128,128]{3,2,1,0:T(8,128)}) fusion(f32[1,28,8,128,128]{4,3,2,1,0:T(8,128)} %param.13), kind=kLoop, calls=%fused_computation.15 | loop fusion | bytes 4194304 | tf_op jit(solution)/shard_map/slice | solution.py:224
  23.7 4.1 %slice_bitcast_fusion.1 = (f32[1,8,128,128]{3,2,1,0:T(8,128)}, f32[1,8,128,128]{3,2,1,0:T(8,128)}, f32[1,8,128,128]{3,2,1,0:T(8,128)S(1)}, f32[1,8,128,128]{3,2,...) fusion(f32[1,28,8,128,128]{4,3,2,1,0:T(8,128)} %param.15, ...), kind=kLoop, calls=%fused_computation.11 | loop fusion | bytes 8388608 | tf_op jit(solution)/shard_map/slice | solution.py:224
  36.9 3.9 %collective-permute-done.7 = bf16[512,128]{1,0:T(8,128)(2,1)S(1)} collective-permute-done((bf16[512,128]{1,0:T(8,128)(2,1)S(1)}, bf16[512,128]{1,0:T(8,128)(2,1)S(1)}, u32[]{:S(2)}, u32[]{:S(2)}) %collective-permute-start.7) | collective-permute-done | bytes 131104 | tf_op jit(solution)/shard_map/ppermute | solution.py:27
  41.5 9.5 %collective-permute-done.9.refs_10_ = bf16[512,1536]{1,0:T(8,128)(2,1)} collective-permute-done((bf16[512,1536]{1,0:T(8,128)(2,1)S(1)}, bf16[512,1536]{1,0:T(8,128)(2,1)}, u32[]{:S(2)}, u32[]{:S(2)}) %collective-permute-start.9) | collective-permute-done | bytes 1572896 | tf_op jit(solution)/shard_map/ppermute | solution.py:46
  51.0 3.0 %collective-permute-start.2 = (bf16[1024,512]{1,0:T(8,128)(2,1)}, bf16[1024,512]{1,0:T(8,128)(2,1)}, u32[]{:S(2)}, u32[]{:S(2)}) collective-permute-start(bf16[1024,512]{1,0:T(8,128)(2,1)} %bitcast.54), channel_id=1, source_target_pairs={{0,24},{8,16},{16,8},{24,0},{1,25},{9,17},{17,9},{25,1},{2,26},{10... | collective-permute-start | bytes 3145736 | tf_op jit(solution)/shard_map/ppermute | solution.py:46
  55.9 19.6 %collective-permute-done.refs_1_ = bf16[1024,512]{1,0:T(8,128)(2,1)S(1)} collective-permute-done((bf16[1024,512]{1,0:T(8,128)(2,1)}, bf16[1024,512]{1,0:T(8,128)(2,1)S(1)}, u32[]{:S(2)}, u32[]{:S(2)}) %collective-permute-start) | collective-permute-done | bytes 1048608 | tf_op jit(solution)/shard_map/ppermute | solution.py:46
  77.1 20.4 %collective-permute-done.2.refs_3_ = bf16[1024,512]{1,0:T(8,128)(2,1)} collective-permute-done((bf16[1024,512]{1,0:T(8,128)(2,1)}, bf16[1024,512]{1,0:T(8,128)(2,1)}, u32[]{:S(2)}, u32[]{:S(2)}) %collective-permute-start.2) | collective-permute-done | bytes 1048608 | tf_op jit(solution)/shard_map/ppermute | solution.py:46
  98.2 2.1 slice.198
  100.2 2.1 slice.199
  102.4 3.8 %collective-permute-done.11.refs_10_ = bf16[512,512]{1,0:T(8,128)(2,1)S(1)} collective-permute-done((bf16[512,512]{1,0:T(8,128)(2,1)S(1)}, bf16[512,512]{1,0:T(8,128)(2,1)S(1)}, u32[]{:S(2)}, u32[]{:S(2)}) %collective-permute-start.11) | collective-permute-done | bytes 524320 | tf_op jit(solution)/shard_map/ppermute | solution.py:46
  106.2 1.7 collective-permute-start.20
  112.6 3.4 %broadcast_select_fusion.1 = (f32[3,8,128,128]{3,2,1,0:T(8,128)S(1)}, f32[3,8,128,128]{3,2,1,0:T(8,128)}) fusion(f32[3,8,128,128]{3,2,1,0:T(8,128)} %collective-permute-done.14, pred[]{:T(512)} %bitcast.7, f32[1,8,128,128]{3,2,1,0:T(8,128)} %get-tuple-element.30, f32[1,8,128,128]{3,2,1,0:T(8,128)} %get-tuple-element.70, f32[1,8,128,128]{3,2,1,0:T(8,128)} %get-tuple-element.38), kind=kLoop, calls=%fused_computation.6 | loop fusion | flops 1179648 | bytes 6291457 | tf_op jit(solution)/shard_map/jit(_where)/select_n | solution.py:219
  119.5 7.5 %collective-permute-done.20.refs_11_ = bf16[256,1536]{1,0:T(8,128)(2,1)} collective-permute-done((bf16[256,1536]{1,0:T(8,128)(2,1)}, bf16[256,1536]{1,0:T(8,128)(2,1)}, u32[]{:S(2)}, u32[]{:S(2)}) %collective-permute-start.20) | collective-permute-done | bytes 786464 | tf_op jit(solution)/shard_map/ppermute | solution.py:46
  127.0 1.7 collective-permute-start.12
  130.2 28.6 %shard_map.103 = (f32[28,8,128,128]{3,2,1,0:T(8,128)}, f32[28,8,128,128]{3,2,1,0:T(8,128)}, f32[28,8,128,128]{3,2,1,0:T(8,128)}) custom-call(s32[224]{0:T(256)S(1)} %and_select_fusion.rows_ref, s32[29]{0:T(128)S(1)} %pad_add_fusion.count_ref, bf16[1024,512]{1,0:T(8,128)(2,1)S(1)} %bitcast.39, bf16[1024,512]{1,0:T(8,128)(2,1)S(1)} %collective-permute-done.refs_1_, ...), custom_call_target="tpu_custom_call" | custom-call | flops 25769803776 | bytes 46137344 | tf_op jit(solution)/shard_map/pallas_call | solution.py:119
  158.9 3.4 %collective-permute-done.17.refs_10_ = bf16[512,1536]{1,0:T(8,128)(2,1)S(1)} collective-permute-done((bf16[512,1536]{1,0:T(8,128)(2,1)S(1)}, bf16[512,1536]{1,0:T(8,128)(2,1)S(1)}, u32[]{:S(2)}, u32[]{:S(2)}) %collective-permute-start.17) | collective-permute-done | bytes 1572896 | tf_op jit(solution)/shard_map/ppermute | solution.py:46
  169.3 1.6 pad_maximum_fusion.refs_13_
  170.8 10.5 %collective-permute-done.18.refs_11_ = bf16[256,1536]{1,0:T(8,128)(2,1)S(1)} collective-permute-done((bf16[256,1536]{1,0:T(8,128)(2,1)S(1)}, bf16[256,1536]{1,0:T(8,128)(2,1)S(1)}, u32[]{:S(2)}, u32[]{:S(2)}) %collective-permute-start.18) | collective-permute-done | bytes 786464 | tf_op jit(solution)/shard_map/ppermute | solution.py:46
  182.5 29.4 %shard_map.104 = (f32[28,8,128,128]{3,2,1,0:T(8,128)}, f32[28,8,128,128]{3,2,1,0:T(8,128)}, f32[28,8,128,128]{3,2,1,0:T(8,128)}) custom-call(s32[224]{0:T(256)S(1)} %and_select_fusion.rows_ref, s32[29]{0:T(128)S(1)} %pad_add_fusion.count_ref, bf16[1024,512]{1,0:T(8,128)(2,1)S(1)} %bitcast.40, ...), custom_call_target="tpu_custom_call", output_to_operand_aliasing={{0}: (18, {}), {1}: (19, {}), {2}: (20, {})} | custom-call | flops 25769803776 | bytes 46137344 | tf_op jit(solution)/shard_map/pallas_call | solution.py:119
  211.9 13.0 %shard_map.105 = (f32[28,8,128,128]{3,2,1,0:T(8,128)}, f32[28,8,128,128]{3,2,1,0:T(8,128)}, f32[28,8,128,128]{3,2,1,0:T(8,128)}) custom-call(s32[224]{0:T(256)S(1)} %and_select_fusion.rows_ref, s32[29]{0:T(128)S(1)} %pad_add_fusion.count_ref, bf16[1024,512]{1,0:T(8,128)(2,1)S(1)} %bitcast.41, ...), custom_call_target="tpu_custom_call", output_to_operand_aliasing={{0}: (18, {}), {1}: (19, {}), {2}: (20, {})} | custom-call | flops 8589934592 | bytes 20971520 | tf_op jit(solution)/shard_map/pallas_call | solution.py:119
  (112 shorter events, 36.3 us)
Async XLA Ops:
  0.6 31.5 %copy-start = (s32[64,224]{1,0:T(8,128)S(1)}, s32[64,224]{1,0:T(8,128)}, u32[]{:S(2)}) copy-start(s32[64,224]{1,0:T(8,128)} %param.10) | copy-start | bytes 172036
  12.8 38.2 %collective-permute-start.9 = (bf16[512,1536]{1,0:T(8,128)(2,1)S(1)}, bf16[512,1536]{1,0:T(8,128)(2,1)}, u32[]{:S(2)}, u32[]{:S(2)}) collective-permute-start(bf16[512,1536]{1,0:T(8,128)(2,1)S(1)} %get-tuple-element.15), channel_id=1, source_target_pairs={{0,16},{8,24},{16,0},{24,8},{1,17},{9,25},{17,1},{25,9},{2,18},{10... | collective-permute-start | bytes 4718600 | tf_op jit(solution)/shard_map/ppermute | solution.py:46
  15.7 39.7 %collective-permute-start.8 = (bf16[512,1536]{1,0:T(8,128)(2,1)S(1)}, bf16[512,1536]{1,0:T(8,128)(2,1)}, u32[]{:S(2)}, u32[]{:S(2)}) collective-permute-start(bf16[512,1536]{1,0:T(8,128)(2,1)S(1)} %get-tuple-element.15), channel_id=1, source_target_pairs={{0,8},{8,0},{16,24},{24,16},{1,9},{9,1},{17,25},{25,17},{2,10},{10... | collective-permute-start | bytes 4718600 | tf_op jit(solution)/shard_map/ppermute | solution.py:46
  17.1 58.3 %collective-permute-start = (bf16[1024,512]{1,0:T(8,128)(2,1)}, bf16[1024,512]{1,0:T(8,128)(2,1)S(1)}, u32[]{:S(2)}, u32[]{:S(2)}) collective-permute-start(bf16[1024,512]{1,0:T(8,128)(2,1)} %bitcast.3), channel_id=1, source_target_pairs={{0,8},{8,0},{16,24},{24,16},{1,9},{9,1},{17,25},{25,17},{2,10},{10... | collective-permute-start | bytes 3145736 | tf_op jit(solution)/shard_map/ppermute | solution.py:46
  18.7 14.5 %collective-permute-start.6 = (bf16[512,128]{1,0:T(8,128)(2,1)S(1)}, bf16[512,128]{1,0:T(8,128)(2,1)S(1)}, u32[]{:S(2)}, u32[]{:S(2)}) collective-permute-start(bf16[512,128]{1,0:T(8,128)(2,1)S(1)} %get-tuple-element.52), channel_id=1, source_target_pairs={{0,7},{1,0},{2,1},{3,2},{4,3},{5,4},{6,5},{7,6},{8,15},{9,8},{10,9... | collective-permute-start | bytes 393224 | tf_op jit(solution)/shard_map/ppermute | solution.py:27
  29.8 67.7 %collective-permute-start.14 = (f32[3,8,128,128]{3,2,1,0:T(8,128)}, f32[3,8,128,128]{3,2,1,0:T(8,128)}, u32[]{:S(2)}, u32[]{:S(2)}) collective-permute-start(f32[3,8,128,128]{3,2,1,0:T(8,128)} %pad_maximum_fusion.3), channel_id=1, source_target_pairs={{0,7},{1,0},{2,1},{3,2},{4,3},{5,4},{6,5},{7,6},{8,15},{9,8},{10,9... | collective-permute-start | bytes 4718600 | tf_op jit(solution)/shard_map/ppermute | solution.py:27
  33.2 7.7 %collective-permute-start.7 = (bf16[512,128]{1,0:T(8,128)(2,1)S(1)}, bf16[512,128]{1,0:T(8,128)(2,1)S(1)}, u32[]{:S(2)}, u32[]{:S(2)}) collective-permute-start(bf16[512,128]{1,0:T(8,128)(2,1)S(1)} %get-tuple-element.53), channel_id=1, source_target_pairs={{0,1},{1,2},{2,3},{3,4},{4,5},{5,6},{6,7},{7,0},{8,9},{9,10},{10,1... | collective-permute-start | bytes 393224 | tf_op jit(solution)/shard_map/ppermute | solution.py:27
  40.9 36.2 %collective-permute-start.1 = (bf16[1024,512]{1,0:T(8,128)(2,1)}, bf16[1024,512]{1,0:T(8,128)(2,1)}, u32[]{:S(2)}, u32[]{:S(2)}) collective-permute-start(bf16[1024,512]{1,0:T(8,128)(2,1)} %bitcast.55), channel_id=1, source_target_pairs={{0,16},{8,24},{16,0},{24,8},{1,17},{9,25},{17,1},{25,9},{2,18},{10... | collective-permute-start | bytes 3145736 | tf_op jit(solution)/shard_map/ppermute | solution.py:46
  51.0 46.5 %collective-permute-start.2 = (bf16[1024,512]{1,0:T(8,128)(2,1)}, bf16[1024,512]{1,0:T(8,128)(2,1)}, u32[]{:S(2)}, u32[]{:S(2)}) collective-permute-start(bf16[1024,512]{1,0:T(8,128)(2,1)} %bitcast.54), channel_id=1, source_target_pairs={{0,24},{8,16},{16,8},{24,0},{1,25},{9,17},{17,9},{25,1},{2,26},{10... | collective-permute-start | bytes 3145736 | tf_op jit(solution)/shard_map/ppermute | solution.py:46
  55.3 54.1 %copy-start.2 = (bf16[512,512]{1,0:T(8,128)(2,1)}, bf16[512,512]{1,0:T(8,128)(2,1)S(1)}, u32[]{:S(2)}) copy-start(bf16[512,512]{1,0:T(8,128)(2,1)S(1)} %pad_maximum_fusion.5.refs_8_) | copy-start | bytes 1572868
  55.3 50.9 %collective-permute-start.11 = (bf16[512,512]{1,0:T(8,128)(2,1)S(1)}, bf16[512,512]{1,0:T(8,128)(2,1)S(1)}, u32[]{:S(2)}, u32[]{:S(2)}) collective-permute-start(bf16[512,512]{1,0:T(8,128)(2,1)S(1)} %pad_maximum_fusion.5.refs_8_), channel_id=1, source_target_pairs={{0,16},{8,24},{16,0},{24,8},{1,17},{9,25},{17,1},{25,9},{2,18},{10... | collective-permute-start | bytes 1572872 | tf_op jit(solution)/shard_map/ppermute | solution.py:46
  75.5 32.5 %collective-permute-start.10 = (bf16[512,512]{1,0:T(8,128)(2,1)S(1)}, bf16[512,512]{1,0:T(8,128)(2,1)S(1)}, u32[]{:S(2)}, u32[]{:S(2)}) collective-permute-start(bf16[512,512]{1,0:T(8,128)(2,1)S(1)} %pad_maximum_fusion.5.refs_8_), channel_id=1, source_target_pairs={{0,8},{8,0},{16,24},{24,16},{1,9},{9,1},{17,25},{25,17},{2,10},{10... | collective-permute-start | bytes 1572872 | tf_op jit(solution)/shard_map/ppermute | solution.py:46
  77.1 40.1 %collective-permute-start.3 = (bf16[1024,512]{1,0:T(8,128)(2,1)S(1)}, bf16[1024,512]{1,0:T(8,128)(2,1)}, u32[]{:S(2)}, u32[]{:S(2)}) collective-permute-start(bf16[1024,512]{1,0:T(8,128)(2,1)S(1)} %collective-permute-done.refs_1_), channel_id=1, source_target_pairs={{0,1},{1,0},{2,3},{3,2},{4,5},{5,4},{6,7},{7,6},{8,9},{9,8},{10,11... | collective-permute-start | bytes 3145736 | tf_op jit(solution)/shard_map/ppermute | solution.py:46
  97.5 21.0 %collective-permute-start.4 = (bf16[1024,512]{1,0:T(8,128)(2,1)}, bf16[1024,512]{1,0:T(8,128)(2,1)}, u32[]{:S(2)}, u32[]{:S(2)}) collective-permute-start(bf16[1024,512]{1,0:T(8,128)(2,1)} %collective-permute-done.1.refs_2_), channel_id=1, source_target_pairs={{0,1},{1,0},{2,3},{3,2},{4,5},{5,4},{6,7},{7,6},{8,9},{9,8},{10,11... | collective-permute-start | bytes 3145736 | tf_op jit(solution)/shard_map/ppermute | solution.py:46
  97.5 22.0 %collective-permute-start.5 = (bf16[1024,512]{1,0:T(8,128)(2,1)}, bf16[1024,512]{1,0:T(8,128)(2,1)}, u32[]{:S(2)}, u32[]{:S(2)}) collective-permute-start(bf16[1024,512]{1,0:T(8,128)(2,1)} %collective-permute-done.2.refs_3_), channel_id=1, source_target_pairs={{0,1},{1,0},{2,3},{3,2},{4,5},{5,4},{6,7},{7,6},{8,9},{9,8},{10,11... | collective-permute-start | bytes 3145736 | tf_op jit(solution)/shard_map/ppermute | solution.py:46
  106.2 20.8 %collective-permute-start.20 = (bf16[256,1536]{1,0:T(8,128)(2,1)}, bf16[256,1536]{1,0:T(8,128)(2,1)}, u32[]{:S(2)}, u32[]{:S(2)}) collective-permute-start(bf16[256,1536]{1,0:T(8,128)(2,1)} %slice.198), channel_id=1, source_target_pairs={{0,8},{8,0},{16,24},{24,16},{1,9},{9,1},{17,25},{25,17},{2,10},{10... | collective-permute-start | bytes 2359304 | tf_op jit(solution)/shard_map/ppermute | solution.py:46
  108.0 20.8 %collective-permute-start.21 = (bf16[256,1536]{1,0:T(8,128)(2,1)}, bf16[256,1536]{1,0:T(8,128)(2,1)}, u32[]{:S(2)}, u32[]{:S(2)}) collective-permute-start(bf16[256,1536]{1,0:T(8,128)(2,1)} %slice.199), channel_id=1, source_target_pairs={{0,16},{8,24},{16,0},{24,8},{1,17},{9,25},{17,1},{25,9},{2,18},{10... | collective-permute-start | bytes 2359304 | tf_op jit(solution)/shard_map/ppermute | solution.py:46
  117.7 44.7 %collective-permute-start.17 = (bf16[512,1536]{1,0:T(8,128)(2,1)S(1)}, bf16[512,1536]{1,0:T(8,128)(2,1)S(1)}, u32[]{:S(2)}, u32[]{:S(2)}) collective-permute-start(bf16[512,1536]{1,0:T(8,128)(2,1)S(1)} %copy-done.22), channel_id=1, source_target_pairs={{0,16},{8,24},{16,0},{24,8},{1,17},{9,25},{17,1},{25,9},{2,18},{10... | collective-permute-start | bytes 4718600 | tf_op jit(solution)/shard_map/ppermute | solution.py:46
  118.5 45.2 %collective-permute-start.16 = (bf16[512,1536]{1,0:T(8,128)(2,1)S(1)}, bf16[512,1536]{1,0:T(8,128)(2,1)S(1)}, u32[]{:S(2)}, u32[]{:S(2)}) collective-permute-start(bf16[512,1536]{1,0:T(8,128)(2,1)S(1)} %copy-done.22), channel_id=1, source_target_pairs={{0,8},{8,0},{16,24},{24,16},{1,9},{9,1},{17,25},{25,17},{2,10},{10... | collective-permute-start | bytes 4718600 | tf_op jit(solution)/shard_map/ppermute | solution.py:46
  119.5 45.2 %collective-permute-start.15 = (f32[3,8,128,128]{3,2,1,0:T(8,128)}, f32[3,8,128,128]{3,2,1,0:T(8,128)S(1)}, u32[]{:S(2)}, u32[]{:S(2)}) collective-permute-start(f32[3,8,128,128]{3,2,1,0:T(8,128)} %get-tuple-element.61), channel_id=1, source_target_pairs={{0,1},{1,2},{2,3},{3,4},{4,5},{5,6},{6,7},{7,0},{8,9},{9,10},{10,1... | collective-permute-start | bytes 4718600 | tf_op jit(solution)/shard_map/ppermute | solution.py:27
  127.0 84.9 %collective-permute-start.12 = (bf16[256,512]{1,0:T(8,128)(2,1)S(1)}, bf16[256,512]{1,0:T(8,128)(2,1)S(1)}, u32[]{:S(2)}, u32[]{:S(2)}) collective-permute-start(bf16[256,512]{1,0:T(8,128)(2,1)S(1)} %slice.188), channel_id=1, source_target_pairs={{0,8},{8,0},{16,24},{24,16},{1,9},{9,1},{17,25},{25,17},{2,10},{10... | collective-permute-start | bytes 786440 | tf_op jit(solution)/shard_map/ppermute | solution.py:46
  128.7 83.1 %collective-permute-start.13 = (bf16[256,512]{1,0:T(8,128)(2,1)S(1)}, bf16[256,512]{1,0:T(8,128)(2,1)S(1)}, u32[]{:S(2)}, u32[]{:S(2)}) collective-permute-start(bf16[256,512]{1,0:T(8,128)(2,1)S(1)} %slice.189), channel_id=1, source_target_pairs={{0,16},{8,24},{16,0},{24,8},{1,17},{9,25},{17,1},{25,9},{2,18},{10... | collective-permute-start | bytes 786440 | tf_op jit(solution)/shard_map/ppermute | solution.py:46
  162.4 18.9 %collective-permute-start.18 = (bf16[256,1536]{1,0:T(8,128)(2,1)S(1)}, bf16[256,1536]{1,0:T(8,128)(2,1)S(1)}, u32[]{:S(2)}, u32[]{:S(2)}) collective-permute-start(bf16[256,1536]{1,0:T(8,128)(2,1)S(1)} %slice.196), channel_id=1, source_target_pairs={{0,8},{8,0},{16,24},{24,16},{1,9},{9,1},{17,25},{25,17},{2,10},{10... | collective-permute-start | bytes 2359304 | tf_op jit(solution)/shard_map/ppermute | solution.py:46
  163.8 18.7 %collective-permute-start.19 = (bf16[256,1536]{1,0:T(8,128)(2,1)S(1)}, bf16[256,1536]{1,0:T(8,128)(2,1)S(1)}, u32[]{:S(2)}, u32[]{:S(2)}) collective-permute-start(bf16[256,1536]{1,0:T(8,128)(2,1)S(1)} %slice.197), channel_id=1, source_target_pairs={{0,16},{8,24},{16,0},{24,8},{1,17},{9,25},{17,1},{25,9},{2,18},{10... | collective-permute-start | bytes 2359304 | tf_op jit(solution)/shard_map/ppermute | solution.py:46
  (21 other events, 87.6 us)
